TPU v7x, 32 devices: a whole 2x2x4 slice. The times are simulated.
32 devices in a mesh: section: 2 (over y), shard: 16 (over z, x, core).
Axes of the slice: x: 2, y: 2, z: 4, core: 2. Of those that a mesh axis runs over, the one named last changes fastest.
Arguments:
- features: bfloat16 [2, 4096, 512], P(None, 'shard'), may hold values from -0.029907227 to 0.029907227
- labels: int32 [2, 4096], P(None, 'shard'), may hold values from 0 to 3
- label_table: float32 [4, 512], replicated, may hold values from -0.01 to 0.01
- tiles: bfloat16 [2, 96, 128, 128], P(None, 'shard'), may hold values from -1 to 1
- tile_rows: int32 [2, 96], P(None, 'shard'), may hold values from 0 to 31, as said below
- tile_cols: int32 [2, 96], P(None, 'shard'), may hold values from 0 to 31, as said below
- tile_live: int32 [2, 16], P(None, 'shard'), may hold values from 2 to 6, as said below
- weights: bfloat16 [2, 512, 512], P('section'), may hold values from -0.25 to 0.25
- gains: bfloat16 [2, 512], P('section'), may hold values from 0 to 1
- head_weight: float32 [512], replicated, may hold values from -0.75 to 0.75
Outputs:
- outcome: float32 [2, 4096], P('section', 'shard')
Inputs may be any that keep to these rules, and one draw needn't show every extreme that they name: `tile_rows`: slot k of shard j has a row block from j * 2 - 1 to (j + 1) * 2. `tile_cols`: slot k of shard j has a column block of that shard's own nodes, j * 2 to (j + 1) * 2 - 1; where its row block is j * 2 - 1 the column block is j * 2, and where its row block is (j + 1) * 2 the column block is (j + 1) * 2 - 1. `tile_live`: in every graph group some shard has all 6 slots live.
All inputs are finite; a program needn't handle non-finite values.
Results may differ from a plain program's by a relative error of at most 0.02.
Values may be sent and summed in bfloat16 or wider, within the bound.
No kernel may reach another device: no remote copies, remote signals or barrier semaphores. Data moves between devices by JAX's collectives and lax.ppermute only.
A program may use at most 64 MiB of HBM per device.

v0:
```python
import jax
import jax.numpy as jnp
from jax import lax
from jax.experimental import pallas as pl
from jax.experimental.pallas import tpu as pltpu
from jax.sharding import PartitionSpec as P

BF16 = jnp.bfloat16
F32 = jnp.float32
PAD = 16
GELU_LINEAR = 2.0 * (2.0 / 3.141592653589793) ** 0.5
GELU_CUBIC = 4.0 * GELU_LINEAR * 0.044715


def split3(value):
    high = value.astype(BF16).astype(F32)
    rest = value - high
    mid = rest.astype(BF16).astype(F32)
    return high, mid, rest - mid


def dot(a, b, dims=((1,), (0,))):
    return lax.dot_general(a, b, (dims, ((), ())), preferred_element_type=F32)


def in_hbm(*arrays):
    return [pltpu.with_memory_space_constraint(array, pltpu.HBM) for array in arrays]


def layer(aggregate, weight, half_gain, state):
    projected = dot(aggregate, weight)
    scale = lax.rsqrt(jnp.mean(projected * projected, axis=-1, keepdims=True) + 1e-06)
    half = (projected * scale * half_gain).astype(BF16)
    inner = half * (BF16(GELU_LINEAR) + BF16(GELU_CUBIC) * (half * half))
    return state + (half + half * jnp.tanh(inner))


def placed(block, blocks, shard, size):
    mirrored = 1 - lax.rem(shard, 2)
    return pl.ds(pl.multiple_of((block + mirrored * (blocks - 1 - 2 * block)) * size, size), size)


def first_kernel(
    tile_rows, tile_cols, tile_live, labels, label_table, tiles, features, weights,
    far, near, crossing, state_out, adjacency_out,
    rows_buf, cols_buf, live_buf, labels_buf, classes_buf, tiles_buf, features_buf, table_buf, sums, sems,
):
    section = lax.axis_index("section")
    shard = lax.axis_index("shard")
    rows, width = features_buf.shape
    slots, size, _ = tiles_buf.shape
    blocks = rows // size
    kept = crossing.shape[0]
    group = section

    small = [(tile_rows, rows_buf), (tile_cols, cols_buf), (tile_live, live_buf)]
    named = [(label_table, classes_buf)]
    spread = []
    for block in range(blocks):
        span, place = pl.ds(block * size, size), placed(block, blocks, shard, size)
        named.append((labels.at[:, span], labels_buf.at[:, place]))
        spread.append((features.at[group, span], features_buf.at[place]))
    half = pl.ds(pl.multiple_of(lax.rem(shard, 2) * kept, kept), kept)
    sent = [(weights.at[0, half], crossing)]
    batches, count = [], 0
    for batch in (small, named, [(tiles.at[group], tiles_buf)], spread, sent):
        batches.append([
            pltpu.make_async_copy(source, target, sems.at[count + index])
            for index, (source, target) in enumerate(batch)
        ])
        count += len(batch)
    for batch in batches:
        for copy in batch:
            copy.start()
    sums[...] = jnp.zeros_like(sums)
    table_buf[...] = jnp.zeros_like(table_buf)

    for copy in batches[1]:
        copy.wait()
    classes = classes_buf.shape[0]
    for part, value in enumerate(split3(classes_buf[...])):
        table_buf[pl.ds(part * classes, classes), :] = value
    depth = table_buf.shape[0]
    index = lax.broadcasted_iota(jnp.int32, (depth, rows), 0)
    wanted = jnp.where(
        index < classes, index,
        jnp.where(index < 2 * classes, index - classes, jnp.where(index < 3 * classes, index - 2 * classes, -1)),
    )
    hot = (wanted == labels_buf[pl.ds(group, 1), :]).astype(F32).astype(BF16)
    embedded = dot(hot, table_buf[...].astype(BF16), ((0,), (0,)))

    for copy in batches[0] + batches[2]:
        copy.wait()
    for slot in range(slots):
        @pl.when(slot < live_buf[0, group])
        def _():
            row = rows_buf[group, slot] - (shard * blocks - 1)
            col = cols_buf[group, slot] - shard * blocks
            sums[placed(row, blocks + 2, shard, size), placed(col, blocks, shard, size)] += tiles_buf[slot].astype(F32)
    adjacency = sums[...].astype(BF16)
    adjacency_out[...] = adjacency

    for copy in batches[3]:
        copy.wait()
    state = (features_buf[...].astype(F32) + embedded).astype(BF16)
    state_out[...] = state
    partial = dot(adjacency[size : size + rows], state).astype(BF16)
    near[:, pl.ds(0, width)] = partial[:size]
    near[:, pl.ds(width, width)] = state[:size]
    near[:, pl.ds(2 * width, size)] = adjacency[:size, :size]
    far[:, pl.ds(0, width)] = partial[rows - size :]
    far[:, pl.ds(width, width)] = state[rows - size :]
    far[:, pl.ds(2 * width, size)] = adjacency[rows + size :, rows - size :]
    for copy in batches[4]:
        copy.wait()


def waiting_kernel(
    adjacency, state, head, gains, weights,
    aggregate, weight, gain, half_gain, head_parts,
    head_buf, parts_buf, sems,
):
    copies = [
        pltpu.make_async_copy(source, target, sems.at[index])
        for index, (source, target) in enumerate(((weights.at[0], weight), (head, head_buf), (gains, gain)))
    ]
    for copy in copies:
        copy.start()
    aggregate[...] = dot(adjacency[...], state[...])
    parts_buf[...] = jnp.zeros_like(parts_buf)
    for copy in copies[1:]:
        copy.wait()
    for part, value in enumerate(split3(head_buf[...])):
        parts_buf[pl.ds(part, 1), :] = value
    head_parts[...] = parts_buf[...].astype(BF16)
    half_gain[...] = 0.5 * gain[...].astype(F32)
    copies[0].wait()


def near_kernel(state, near, aggregate, weight, half_gain, near_blocks):
    size, width = near.shape[0], state.shape[1]
    near_state = near[:, pl.ds(width, width)]
    first_sum = aggregate[pl.ds(0, size), :] + near[:, pl.ds(0, width)].astype(F32)
    next_sum = aggregate[pl.ds(size, size), :] + dot(near[:, pl.ds(2 * width, size)], near_state)
    near_blocks[pl.ds(0, size), :] = first_sum.astype(BF16)
    near_blocks[pl.ds(size, size), :] = next_sum.astype(BF16)

    @pl.when(lax.axis_index("section") == 0)
    def _():
        for place, block in enumerate((near_state, state[pl.ds(0, size), :])):
            span = pl.ds(place * size, size)
            near_blocks[span, :] = layer(near_blocks[span, :], weight[...], half_gain[...], block)


def second_kernel(
    adjacency, state, far, near, other_gain, crossed, relayed, near_blocks, aggregate, own_weight, half_gain, head_parts,
    outcome,
    mats, aggregates, states, next_states,
):
    first = lax.axis_index("section") == 0
    shard = lax.axis_index("shard")
    even = lax.rem(shard, 2) == 0
    rows, width = state.shape
    size = near.shape[0]
    kept = crossed.shape[0]
    total = rows + 2 * size
    inside, last = pl.ds(size, rows), pl.ds(size + rows, size)

    for place, (one, two) in enumerate(((crossed, relayed), (relayed, crossed))):
        span = pl.ds(place * kept, kept)
        own = own_weight[span, :]
        got = jnp.where(even, one[...], two[...])
        mats[0, span, :] = jnp.where(first, own, got)
        mats[1, span, :] = jnp.where(first, got, own)
    got = 0.5 * other_gain[...].astype(F32)
    gain = (jnp.where(first, half_gain[...], got), jnp.where(first, got, half_gain[...]))

    near_tile, far_tile = near[:, pl.ds(2 * width, size)], far[:, pl.ds(2 * width, size)]
    far_state = far[:, pl.ds(width, width)]
    states[inside, :] = state[...]
    states[last, :] = far_state
    for start in range(2 * size, rows, size):
        aggregates[pl.ds(start, size), :] = aggregate[pl.ds(start, size), :].astype(BF16)
    edge = pl.ds(rows, size)
    aggregates[edge, :] = (aggregate[edge, :] + dot(far_tile, far_state)).astype(BF16)
    aggregates[last, :] = (
        aggregate[last, :] + far[:, pl.ds(0, width)].astype(F32)
    ).astype(BF16)

    def step(start, source):
        span = pl.ds(start, size)
        next_states[span, :] = layer(source[span, :], mats[0], gain[0], states[span, :])

    @pl.when(first)
    def _():
        next_states[pl.ds(0, 2 * size), :] = near_blocks[...]

    @pl.when(jnp.logical_not(first))
    def _():
        states[pl.ds(0, size), :] = near[:, pl.ds(width, width)]
        step(0, near_blocks)
        step(size, near_blocks)

    for start in range(2 * size, total, size):
        step(start, aggregates)

    inner = dot(adjacency[inside, :], next_states[inside, :])
    inner = jnp.concatenate(
        [
            inner[:size] + dot(near_tile, next_states[pl.ds(0, size), :]),
            *([inner[size : rows - size]] if rows > 2 * size else []),
            inner[rows - size :] + dot(far_tile, next_states[last, :]),
        ],
        axis=0,
    ).astype(BF16)
    state = jnp.concatenate(
        [
            layer(inner[start : start + size], mats[1], gain[1], next_states[pl.ds(size + start, size), :])
            for start in range(0, rows, size)
        ],
        axis=0,
    )
    scores = dot(head_parts[...], state, ((1,), (1,)))
    scores = scores[0:1] + scores[1:2] + scores[2:3]
    for block in range(rows // size):
        outcome[:, placed(block, rows // size, shard, size)] = scores[:, block * size : (block + 1) * size]


def paired(features, labels, label_table, tiles, tile_rows, tile_cols, tile_live, weights, gains, head_weight):
    shard_count = lax.axis_size("shard")
    groups, rows, width = features.shape
    _, slots, size, _ = tiles.shape
    depth = weights.shape[1]
    kept = depth // 2
    classes = label_table.shape[0]
    message = jax.ShapeDtypeStruct((size, 2 * width + size), BF16)
    vmem = pl.BlockSpec(memory_space=pltpu.VMEM)
    hbm = pl.BlockSpec(memory_space=pltpu.HBM)
    table_rows = -(-3 * classes // PAD) * PAD

    far, near, crossing, state, adjacency = pl.pallas_call(
        first_kernel,
        out_shape=(
            message,
            message,
            jax.ShapeDtypeStruct((kept, width), BF16),
            jax.ShapeDtypeStruct((rows, width), BF16),
            jax.ShapeDtypeStruct((rows + 2 * size, rows), BF16),
        ),
        in_specs=[hbm] * 8,
        out_specs=(vmem,) * 5,
        scratch_shapes=[
            pltpu.SMEM((groups, slots), jnp.int32),
            pltpu.SMEM((groups, slots), jnp.int32),
            pltpu.SMEM((1, groups), jnp.int32),
            pltpu.VMEM((groups, rows), jnp.int32),
            pltpu.VMEM((classes, width), F32),
            pltpu.VMEM((slots, size, size), BF16),
            pltpu.VMEM((rows, width), BF16),
            pltpu.VMEM((table_rows, width), F32),
            pltpu.VMEM((rows + 2 * size, rows), F32),
            pltpu.SemaphoreType.DMA((6 + 2 * (rows // size),)),
        ],
        compiler_params=pltpu.CompilerParams(vmem_limit_bytes=16 * 2**20),
        name="messages",
    )(*in_hbm(tile_rows, tile_cols, tile_live.T, labels, label_table, tiles, features, weights))

    beside = [(i, i ^ 1) for i in range(shard_count)]
    apart = [(i, (i + 1) % shard_count) for i in range(1, shard_count, 2)]
    apart += [(b, a) for a, b in apart]
    across = [(0, 1), (1, 0)]
    crossed = lax.ppermute(crossing, "section", across)
    far = lax.ppermute(far, "shard", apart)
    near = lax.ppermute(near, "shard", beside)

    aggregate, own_weight, gain, half_gain, head_parts = pl.pallas_call(
        waiting_kernel,
        out_shape=(
            jax.ShapeDtypeStruct((rows + 2 * size, width), F32),
            jax.ShapeDtypeStruct((depth, width), BF16),
            jax.ShapeDtypeStruct((1, width), BF16),
            jax.ShapeDtypeStruct((1, width), F32),
            jax.ShapeDtypeStruct((PAD, width), BF16),
        ),
        in_specs=[vmem] * 2 + [hbm] * 3,
        out_specs=(vmem,) * 5,
        scratch_shapes=[
            pltpu.VMEM((1, width), F32),
            pltpu.VMEM((PAD, width), F32),
            pltpu.SemaphoreType.DMA((3,)),
        ],
        compiler_params=pltpu.CompilerParams(vmem_limit_bytes=16 * 2**20),
        cost_estimate=pl.CostEstimate(flops=4 * 10**9, bytes_accessed=2**20, transcendentals=0),
        name="waiting",
    )(adjacency, state, *in_hbm(head_weight.reshape(1, width), gains, weights))

    other_gain = lax.ppermute(gain, "section", across)
    near_blocks = pl.pallas_call(
        near_kernel,
        out_shape=jax.ShapeDtypeStruct((2 * size, width), BF16),
        in_specs=[vmem] * 5,
        out_specs=vmem,
        compiler_params=pltpu.CompilerParams(vmem_limit_bytes=16 * 2**20),
        name="beside",
    )(state, near, aggregate, own_weight, half_gain)

    crossed, near_blocks, other_gain = lax.optimization_barrier((crossed, near_blocks, other_gain))
    relayed = lax.ppermute(crossed, "shard", beside)

    return pl.pallas_call(
        second_kernel,
        out_shape=jax.ShapeDtypeStruct((1, rows), F32),
        in_specs=[vmem] * 12,
        out_specs=vmem,
        scratch_shapes=[
            pltpu.VMEM((2, depth, width), BF16),
            pltpu.VMEM((rows + 2 * size, width), BF16),
            pltpu.VMEM((rows + 2 * size, width), BF16),
            pltpu.VMEM((rows + 2 * size, width), BF16),
        ],
        compiler_params=pltpu.CompilerParams(vmem_limit_bytes=32 * 2**20),
        name="layers",
    )(
        adjacency, state, far, near, other_gain, crossed, relayed,
        near_blocks, aggregate, own_weight, half_gain, head_parts,
    )


def extended_2(block, sides, width):
    for axis, dim in sides:
        count = lax.axis_size(axis)
        forward = [(i, i + 1) for i in range(count - 1)]
        backward = [(target, source) for source, target in forward]
        low = lax.ppermute(
            lax.slice_in_dim(block, block.shape[dim] - width, None, axis=dim), axis, forward
        )
        high = lax.ppermute(lax.slice_in_dim(block, 0, width, axis=dim), axis, backward)
        block = jnp.concatenate([low, block, high], axis=dim)
    return block


def body(
    features,
    labels,
    label_table,
    tiles,
    tile_rows,
    tile_cols,
    tile_live,
    weights,
    gains,
    head_weight,
):
    section_count = lax.axis_size("section")
    section_index = lax.axis_index("section")
    shard_index = lax.axis_index("shard")
    batch_count = features.shape[0]
    row_count = features.shape[1]
    feature_width = features.shape[2]
    tile_size = tiles.shape[2]
    slot_count = tiles.shape[1]
    label_count = label_table.shape[0]
    per_rows = row_count // tile_size
    per_section = batch_count // section_count
    slot_ids = jnp.arange(slot_count, dtype=jnp.int32)
    place_ids = jnp.arange(per_rows + 2, dtype=jnp.int32)

    def apply_layer(state, parts, layer_weight, layer_gain):
        group_tiles, col_local, placing, from_below, from_above = parts
        block_view = state.reshape(per_rows, tile_size, feature_width)
        chosen_blocks = jnp.take(block_view, col_local, axis=0)
        products = jnp.einsum(
            "kab,kbd->kad", group_tiles, chosen_blocks, preferred_element_type=jnp.float32
        )
        partial_value = jnp.einsum(
            "kp,kad->pad", placing, products, precision=lax.Precision.HIGHEST
        )
        edge_states = jnp.concatenate([state[:tile_size], state[row_count - tile_size :]], axis=0)
        extended = extended_2(edge_states, (("shard", 0),), tile_size)
        below_block = extended[:tile_size].astype(jnp.float32)
        above_block = extended[extended.shape[0] - tile_size :].astype(jnp.float32)
        own_rows = partial_value.reshape(row_count, feature_width)
        own_rows = own_rows.at[:tile_size].add(
            jnp.dot(from_below, below_block, precision=lax.Precision.HIGHEST)
        )
        own_rows = own_rows.at[row_count - tile_size :].add(
            jnp.dot(from_above, above_block, precision=lax.Precision.HIGHEST)
        )
        aggregate = own_rows.astype(jnp.bfloat16)
        projected = jnp.dot(aggregate, layer_weight, preferred_element_type=jnp.float32)
        scale = lax.rsqrt(jnp.mean(projected * projected, axis=-1, keepdims=True) + 1e-06)
        normed = projected * scale * layer_gain.astype(jnp.float32)
        return (state.astype(jnp.float32) + jax.nn.gelu(normed)).astype(jnp.bfloat16)

    layer_mats, layer_gains = (
        lax.all_gather(weights, "section", axis=0, tiled=True),
        lax.all_gather(gains, "section", axis=0, tiled=True),
    )
    batch_index = section_index * per_section + 0
    group_tiles = lax.dynamic_index_in_dim(tiles, batch_index, 0, keepdims=False)
    group_rows = lax.dynamic_index_in_dim(tile_rows, batch_index, 0, keepdims=False)
    group_cols = lax.dynamic_index_in_dim(tile_cols, batch_index, 0, keepdims=False)
    group_live = lax.dynamic_index_in_dim(tile_live, batch_index, 0, keepdims=False)
    col_local = group_cols - shard_index * per_rows
    slot_local = group_rows - (shard_index * per_rows - 1)
    live_mask = (slot_ids < group_live[0]).astype(jnp.float32)
    placing = (slot_local[:, None] == place_ids[None, :]).astype(jnp.float32) * live_mask[:, None]
    edge_pick = jnp.stack([placing[:, 0], placing[:, per_rows + 1]], axis=1)
    edge_tiles = jnp.einsum(
        "kp,kab->pab", edge_pick, group_tiles.astype(jnp.float32), precision=lax.Precision.HIGHEST
    )
    received = extended_2(edge_tiles, (("shard", 0),), 1)
    parts = (group_tiles, col_local, placing[:, 1 : per_rows + 1], received[0], received[3])

    def through(layer_index, state):
        return apply_layer(state, parts, layer_mats[layer_index], layer_gains[layer_index])

    group_labels = lax.dynamic_index_in_dim(labels, batch_index, 0, keepdims=False)
    group_features = lax.dynamic_index_in_dim(features, batch_index, 0, keepdims=False)
    labels_hot = (
        group_labels[:, None] == jnp.arange(label_count, dtype=jnp.int32)[None, :]
    ).astype(jnp.float32)
    embedded = jnp.dot(labels_hot, label_table, precision=lax.Precision.HIGHEST)
    state = lax.fori_loop(
        0,
        section_count,
        through,
        (group_features.astype(jnp.float32) + embedded).astype(jnp.bfloat16),
    )
    results = [jnp.dot(state.astype(jnp.float32), head_weight, precision=lax.Precision.HIGHEST)]
    return jnp.stack(results)


def solution(mesh):
    return jax.shard_map(
        paired if mesh.shape["section"] == 2 else body,
        mesh=mesh,
        in_specs=(
            P(None, "shard", None),
            P(None, "shard"),
            P(),
            P(None, "shard", None, None),
            P(None, "shard"),
            P(None, "shard"),
            P(None, "shard"),
            P("section", None, None),
            P("section", None),
            P(),
        ),
        out_specs=P("section", "shard"),
        check_vma=False,
    )
```

profile of v0, /device:TPU:0, one launch (start us, length us, event | category | flops | bytes accessed | tf_op | source)
XLA Modules:
  0.0 16.6 jit_solution(13956768607638476250)
XLA Ops:
  0.0 1.5 %messages.1 = (bf16[128,1152]{1,0:T(8,128)(2,1)S(1)}, bf16[128,1152]{1,0:T(8,128)(2,1)S(1)}, bf16[256,512]{1,0:T(8,128)(2,1)S(1)}, bf16[256,512]{1,0:T(8,128)(2,1)S(1)}, bf16[512,256]{1,0:T(8,128)(2,1)S(1)}) custom-call(s32[2,6]{1,0:T(2,128)} %tile_rows.1, s32[2,6]{1,0:T(2,128)} %tile_cols.1, s32[1,2]{1,0:T(1,128)} %bitcast.2, s32[2,256]{1,0:T(2,128)} %labels.1, ...), custom_call_target="tpu_custom_call" | custom-call | tf_op jit(solution)/shard_map/messages/pallas_call | solution.py:241
  1.5 3.1 %collective-permute-start.2 = (bf16[256,512]{1,0:T(8,128)(2,1)S(1)}, bf16[256,512]{1,0:T(8,128)(2,1)S(1)}, u32[]{:S(2)}, u32[]{:S(2)}) collective-permute-start(bf16[256,512]{1,0:T(8,128)(2,1)S(1)} %get-tuple-element.22), channel_id=1, source_target_pairs={{0,16},{16,0},{1,17},{17,1},{2,18},{18,2},{3,19},{19,3},{4,20},{20... | collective-permute-start | bytes 786440 | tf_op jit(solution)/shard_map/ppermute | solution.py:272
  4.5 3.7 %collective-permute-start = (bf16[128,1152]{1,0:T(8,128)(2,1)S(1)}, bf16[128,1152]{1,0:T(8,128)(2,1)S(1)}, u32[]{:S(2)}, u32[]{:S(2)}) collective-permute-start(bf16[128,1152]{1,0:T(8,128)(2,1)S(1)} %get-tuple-element.20), channel_id=1, source_target_pairs={{1,2},{3,4},{5,6},{7,8},{9,10},{11,12},{13,14},{15,0},{2,1},{4,3},... | collective-permute-start | bytes 884744 | tf_op jit(solution)/shard_map/ppermute | solution.py:273
  8.2 0.0 collective-permute-start.1
  8.2 1.1 %waiting.1 = (f32[512,512]{1,0:T(8,128)S(1)}, bf16[512,512]{1,0:T(8,128)(2,1)S(1)}, bf16[1,512]{1,0:T(2,128)(2,1)S(1)}, f32[1,512]{1,0:T(1,128)S(1)}, bf16[16,512]{1,0:T(8,128)(2,1)S(1)}) custom-call(bf16[512,256]{1,0:T(8,128)(2,1)S(1)} %get-tuple-element.18.adjacency, bf16[256,512]{1,0:T(8,128)(2,1)S(1)} %get-tuple-element.19.state, f32[1,512]{1,0:T(1,128)} %bitcast.3, ...), custom_call_target="tpu_custom_call" | custom-call | flops 4000000000 | bytes 1048576 | tf_op jit(solution)/shard_map/waiting/pallas_call | solution.py:276
  9.3 0.6 %collective-permute-start.3 = (bf16[1,512]{1,0:T(2,128)(2,1)S(1)}, bf16[1,512]{1,0:T(2,128)(2,1)S(1)}, u32[]{:S(2)}, u32[]{:S(2)}) collective-permute-start(bf16[1,512]{1,0:T(2,128)(2,1)S(1)} %get-tuple-element.26), channel_id=1, source_target_pairs={{0,16},{16,0},{1,17},{17,1},{2,18},{18,2},{3,19},{19,3},{4,20},{20... | collective-permute-start | bytes 3080 | tf_op jit(solution)/shard_map/ppermute | solution.py:297
  9.9 0.0 collective-permute-done.1.near
  9.9 0.6 %beside.1.near_blocks = bf16[256,512]{1,0:T(8,128)(2,1)S(1)} custom-call(bf16[256,512]{1,0:T(8,128)(2,1)S(1)} %get-tuple-element.19.state, bf16[128,1152]{1,0:T(8,128)(2,1)S(1)} %collective-permute-done.1.near, f32[512,512]{1,0:T(8,128)S(1)} %get-tuple-element.23.aggregate, bf16[512,512]{1,0:T(8,128)(2,1)S(1)} %get-tuple-element.24.weight.own_weight, ...), custom_call_target="tpu_custom_call" | custom-call | tf_op jit(solution)/shard_map/beside/pallas_call | solution.py:298
  10.5 2.4 %collective-permute-done.3.other_gain = bf16[1,512]{1,0:T(2,128)(2,1)S(1)} collective-permute-done((bf16[1,512]{1,0:T(2,128)(2,1)S(1)}, bf16[1,512]{1,0:T(2,128)(2,1)S(1)}, u32[]{:S(2)}, u32[]{:S(2)}) %collective-permute-start.3) | collective-permute-done | bytes 1056 | tf_op jit(solution)/shard_map/ppermute | solution.py:297
  12.9 0.0 collective-permute-done.2.crossed
  12.9 0.0 collective-permute-start.4
  12.9 0.5 %collective-permute-done.far = bf16[128,1152]{1,0:T(8,128)(2,1)S(1)} collective-permute-done((bf16[128,1152]{1,0:T(8,128)(2,1)S(1)}, bf16[128,1152]{1,0:T(8,128)(2,1)S(1)}, u32[]{:S(2)}, u32[]{:S(2)}) %collective-permute-start) | collective-permute-done | bytes 294944 | tf_op jit(solution)/shard_map/ppermute | solution.py:273
  13.5 1.0 %collective-permute-done.4.relayed = bf16[256,512]{1,0:T(8,128)(2,1)S(1)} collective-permute-done((bf16[256,512]{1,0:T(8,128)(2,1)S(1)}, bf16[256,512]{1,0:T(8,128)(2,1)S(1)}, u32[]{:S(2)}, u32[]{:S(2)}) %collective-permute-start.4) | collective-permute-done | bytes 262176 | tf_op jit(solution)/shard_map/ppermute | solution.py:308
  14.5 2.1 %layers.1 = f32[1,256]{1,0:T(1,128)} custom-call(bf16[512,256]{1,0:T(8,128)(2,1)S(1)} %get-tuple-element.18.adjacency, bf16[256,512]{1,0:T(8,128)(2,1)S(1)} %get-tuple-element.19.state, bf16[128,1152]{1,0:T(8,128)(2,1)S(1)} %collective-permute-done.far, bf16[128,1152]{1,0:T(8,128)(2,1)S(1)} %collective-permute-done.1.near, ...), custom_call_target="tpu_custom_call" | custom-call | tf_op jit(solution)/shard_map/layers/pallas_call | solution.py:310
Async XLA Ops:
  1.5 11.5 %collective-permute-start.2 = (bf16[256,512]{1,0:T(8,128)(2,1)S(1)}, bf16[256,512]{1,0:T(8,128)(2,1)S(1)}, u32[]{:S(2)}, u32[]{:S(2)}) collective-permute-start(bf16[256,512]{1,0:T(8,128)(2,1)S(1)} %get-tuple-element.22), channel_id=1, source_target_pairs={{0,16},{16,0},{1,17},{17,1},{2,18},{18,2},{3,19},{19,3},{4,20},{20... | collective-permute-start | bytes 786440 | tf_op jit(solution)/shard_map/ppermute | solution.py:272
  4.5 9.0 %collective-permute-start = (bf16[128,1152]{1,0:T(8,128)(2,1)S(1)}, bf16[128,1152]{1,0:T(8,128)(2,1)S(1)}, u32[]{:S(2)}, u32[]{:S(2)}) collective-permute-start(bf16[128,1152]{1,0:T(8,128)(2,1)S(1)} %get-tuple-element.20), channel_id=1, source_target_pairs={{1,2},{3,4},{5,6},{7,8},{9,10},{11,12},{13,14},{15,0},{2,1},{4,3},... | collective-permute-start | bytes 884744 | tf_op jit(solution)/shard_map/ppermute | solution.py:273
  8.2 1.7 %collective-permute-start.1 = (bf16[128,1152]{1,0:T(8,128)(2,1)S(1)}, bf16[128,1152]{1,0:T(8,128)(2,1)S(1)}, u32[]{:S(2)}, u32[]{:S(2)}) collective-permute-start(bf16[128,1152]{1,0:T(8,128)(2,1)S(1)} %get-tuple-element.21), channel_id=1, source_target_pairs={{0,1},{1,0},{2,3},{3,2},{4,5},{5,4},{6,7},{7,6},{8,9},{9,8},{10,11... | collective-permute-start | bytes 884744 | tf_op jit(solution)/shard_map/ppermute | solution.py:274
  9.3 3.7 %collective-permute-start.3 = (bf16[1,512]{1,0:T(2,128)(2,1)S(1)}, bf16[1,512]{1,0:T(2,128)(2,1)S(1)}, u32[]{:S(2)}, u32[]{:S(2)}) collective-permute-start(bf16[1,512]{1,0:T(2,128)(2,1)S(1)} %get-tuple-element.26), channel_id=1, source_target_pairs={{0,16},{16,0},{1,17},{17,1},{2,18},{18,2},{3,19},{19,3},{4,20},{20... | collective-permute-start | bytes 3080 | tf_op jit(solution)/shard_map/ppermute | solution.py:297
  12.9 1.5 %collective-permute-start.4 = (bf16[256,512]{1,0:T(8,128)(2,1)S(1)}, bf16[256,512]{1,0:T(8,128)(2,1)S(1)}, u32[]{:S(2)}, u32[]{:S(2)}) collective-permute-start(bf16[256,512]{1,0:T(8,128)(2,1)S(1)} %collective-permute-done.2.crossed), channel_id=1, source_target_pairs={{0,1},{1,0},{2,3},{3,2},{4,5},{5,4},{6,7},{7,6},{8,9},{9,8},{10,11... | collective-permute-start | bytes 786440 | tf_op jit(solution)/shard_map/ppermute | solution.py:308
where the time goes:
time: 16.7 us; the launch traced here: 16.6 us
  starting transfers between devices  7.29 us (44%)
  Pallas kernels  5.27 us (32%)
  waiting for transfers between devices  3.96 us (24%)
    ppermute x1, starting transfers between devices, paired(): far = lax.ppermute(far, 'shard', apart)  3.65 us
    ppermute x1, starting transfers between devices, paired(): crossed = lax.ppermute(crossing, 'section', across)  3.06 us
    ppermute x1, waiting for transfers between devices, paired(): other_gain = lax.ppermute(gain, 'section', across)  2.42 us
    pallas_call x1, Pallas kernels, paired(): pl.pallas_call(second_kernel, out_shape=jax.ShapeDtypeStruct((1, rows), F...  2.09 us
    pallas_call x1, Pallas kernels, paired(): pl.pallas_call(first_kernel, out_shape=(message, message, jax.ShapeDtypeS...  1.46 us
    pallas_call x1, Pallas kernels, paired(): pl.pallas_call(waiting_kernel, out_shape=(jax.ShapeDtypeStruct((rows + 2...  1.08 us
    ppermute x1, waiting for transfers between devices, paired(): relayed = lax.ppermute(crossed, 'shard', beside)  0.99 us
    pallas_call x1, Pallas kernels, paired(): pl.pallas_call(near_kernel, out_shape=jax.ShapeDtypeStruct((2 * size, wid...  0.64 us
  transfers between devices with their start and end apart: 5, of which 3 were waited for; matrix products, arithmetic and copies ran while one was open for 0% of the time, Pallas kernels for 10%

commit v1 on v0

--- a/solution.py
+++ b/solution.py
@@ -8,6 +8,7 @@
 BF16 = jnp.bfloat16
 F32 = jnp.float32
 PAD = 16
+EXTRA = 8
 GELU_LINEAR = 2.0 * (2.0 / 3.141592653589793) ** 0.5
 GELU_CUBIC = 4.0 * GELU_LINEAR * 0.044715
 
@@ -41,16 +42,16 @@
 
 
 def first_kernel(
-    tile_rows, tile_cols, tile_live, labels, label_table, tiles, features, weights,
+    tile_rows, tile_cols, tile_live, labels, label_table, tiles, features, gains, weights,
     far, near, crossing, state_out, adjacency_out,
-    rows_buf, cols_buf, live_buf, labels_buf, classes_buf, tiles_buf, features_buf, table_buf, sums, sems,
+    rows_buf, cols_buf, live_buf, labels_buf, classes_buf, tiles_buf, features_buf, gains_buf, table_buf, sums, sems,
 ):
     section = lax.axis_index("section")
     shard = lax.axis_index("shard")
     rows, width = features_buf.shape
     slots, size, _ = tiles_buf.shape
     blocks = rows // size
-    kept = crossing.shape[0]
+    kept = crossing.shape[0] - EXTRA
     group = section
 
     small = [(tile_rows, rows_buf), (tile_cols, cols_buf), (tile_live, live_buf)]
@@ -61,7 +62,7 @@
         named.append((labels.at[:, span], labels_buf.at[:, place]))
         spread.append((features.at[group, span], features_buf.at[place]))
     half = pl.ds(pl.multiple_of(lax.rem(shard, 2) * kept, kept), kept)
-    sent = [(weights.at[0, half], crossing)]
+    sent = [(gains, gains_buf), (weights.at[0, half], crossing.at[pl.ds(0, kept)])]
     batches, count = [], 0
     for batch in (small, named, [(tiles.at[group], tiles_buf)], spread, sent):
         batches.append([
@@ -111,18 +112,19 @@
     far[:, pl.ds(0, width)] = partial[rows - size :]
     far[:, pl.ds(width, width)] = state[rows - size :]
     far[:, pl.ds(2 * width, size)] = adjacency[rows + size :, rows - size :]
-    for copy in batches[4]:
-        copy.wait()
+    batches[4][0].wait()
+    crossing[pl.ds(kept, EXTRA), :] = jnp.broadcast_to(gains_buf[...].astype(F32), (EXTRA, width)).astype(BF16)
+    batches[4][1].wait()
 
 
 def waiting_kernel(
     adjacency, state, head, gains, weights,
-    aggregate, weight, gain, half_gain, head_parts,
-    head_buf, parts_buf, sems,
+    aggregate, weight, half_gain, head_parts,
+    head_buf, gains_buf, parts_buf, sems,
 ):
     copies = [
         pltpu.make_async_copy(source, target, sems.at[index])
-        for index, (source, target) in enumerate(((weights.at[0], weight), (head, head_buf), (gains, gain)))
+        for index, (source, target) in enumerate(((weights.at[0], weight), (head, head_buf), (gains, gains_buf)))
     ]
     for copy in copies:
         copy.start()
@@ -133,76 +135,59 @@
     for part, value in enumerate(split3(head_buf[...])):
         parts_buf[pl.ds(part, 1), :] = value
     head_parts[...] = parts_buf[...].astype(BF16)
-    half_gain[...] = 0.5 * gain[...].astype(F32)
+    half_gain[...] = 0.5 * gains_buf[...].astype(F32)
     copies[0].wait()
 
 
-def near_kernel(state, near, aggregate, weight, half_gain, near_blocks):
-    size, width = near.shape[0], state.shape[1]
-    near_state = near[:, pl.ds(width, width)]
-    first_sum = aggregate[pl.ds(0, size), :] + near[:, pl.ds(0, width)].astype(F32)
-    next_sum = aggregate[pl.ds(size, size), :] + dot(near[:, pl.ds(2 * width, size)], near_state)
-    near_blocks[pl.ds(0, size), :] = first_sum.astype(BF16)
-    near_blocks[pl.ds(size, size), :] = next_sum.astype(BF16)
-
-    @pl.when(lax.axis_index("section") == 0)
-    def _():
-        for place, block in enumerate((near_state, state[pl.ds(0, size), :])):
-            span = pl.ds(place * size, size)
-            near_blocks[span, :] = layer(near_blocks[span, :], weight[...], half_gain[...], block)
+def near_kernel(near, aggregate, near_aggregate):
+    size, width = near.shape[0], aggregate.shape[1]
+    first, second = pl.ds(0, size), pl.ds(size, size)
+    near_aggregate[first, :] = (aggregate[first, :] + near[:, pl.ds(0, width)].astype(F32)).astype(BF16)
+    near_aggregate[second, :] = (
+        aggregate[second, :] + dot(near[:, pl.ds(2 * width, size)], near[:, pl.ds(width, width)])
+    ).astype(BF16)
 
 
 def second_kernel(
-    adjacency, state, far, near, other_gain, crossed, relayed, near_blocks, aggregate, own_weight, half_gain, head_parts,
+    adjacency, state, far, near, crossed, relayed, near_aggregate, aggregate, own_weight, half_gain, head_parts,
     outcome,
-    mats, aggregates, states, next_states,
+    mats, aggregates, next_states,
 ):
     first = lax.axis_index("section") == 0
     shard = lax.axis_index("shard")
     even = lax.rem(shard, 2) == 0
     rows, width = state.shape
     size = near.shape[0]
-    kept = crossed.shape[0]
+    kept = crossed.shape[0] - EXTRA
     total = rows + 2 * size
     inside, last = pl.ds(size, rows), pl.ds(size + rows, size)
 
     for place, (one, two) in enumerate(((crossed, relayed), (relayed, crossed))):
         span = pl.ds(place * kept, kept)
         own = own_weight[span, :]
-        got = jnp.where(even, one[...], two[...])
+        got = jnp.where(even, one[pl.ds(0, kept), :], two[pl.ds(0, kept), :])
         mats[0, span, :] = jnp.where(first, own, got)
         mats[1, span, :] = jnp.where(first, got, own)
-    got = 0.5 * other_gain[...].astype(F32)
+    got = 0.5 * crossed[pl.ds(kept, EXTRA), :].astype(F32)[0:1]
     gain = (jnp.where(first, half_gain[...], got), jnp.where(first, got, half_gain[...]))
 
     near_tile, far_tile = near[:, pl.ds(2 * width, size)], far[:, pl.ds(2 * width, size)]
-    far_state = far[:, pl.ds(width, width)]
-    states[inside, :] = state[...]
-    states[last, :] = far_state
+    edge = pl.ds(rows, size)
     for start in range(2 * size, rows, size):
         aggregates[pl.ds(start, size), :] = aggregate[pl.ds(start, size), :].astype(BF16)
-    edge = pl.ds(rows, size)
-    aggregates[edge, :] = (aggregate[edge, :] + dot(far_tile, far_state)).astype(BF16)
-    aggregates[last, :] = (
-        aggregate[last, :] + far[:, pl.ds(0, width)].astype(F32)
-    ).astype(BF16)
-
-    def step(start, source):
+    aggregates[edge, :] = (aggregate[edge, :] + dot(far_tile, far[:, pl.ds(width, width)])).astype(BF16)
+    aggregates[last, :] = (aggregate[last, :] + far[:, pl.ds(0, width)].astype(F32)).astype(BF16)
+
+    for start in range(0, total, size):
         span = pl.ds(start, size)
-        next_states[span, :] = layer(source[span, :], mats[0], gain[0], states[span, :])
-
-    @pl.when(first)
-    def _():
-        next_states[pl.ds(0, 2 * size), :] = near_blocks[...]
-
-    @pl.when(jnp.logical_not(first))
-    def _():
-        states[pl.ds(0, size), :] = near[:, pl.ds(width, width)]
-        step(0, near_blocks)
-        step(size, near_blocks)
-
-    for start in range(2 * size, total, size):
-        step(start, aggregates)
+        source = near_aggregate if start < 2 * size else aggregates
+        if start == 0:
+            before = near[:, pl.ds(width, width)]
+        elif start < total - size:
+            before = state[pl.ds(start - size, size), :]
+        else:
+            before = far[:, pl.ds(width, width)]
+        next_states[span, :] = layer(source[span, :], mats[0], gain[0], before)
 
     inner = dot(adjacency[inside, :], next_states[inside, :])
     inner = jnp.concatenate(
@@ -243,11 +228,11 @@
         out_shape=(
             message,
             message,
-            jax.ShapeDtypeStruct((kept, width), BF16),
+            jax.ShapeDtypeStruct((kept + EXTRA, width), BF16),
             jax.ShapeDtypeStruct((rows, width), BF16),
             jax.ShapeDtypeStruct((rows + 2 * size, rows), BF16),
         ),
-        in_specs=[hbm] * 8,
+        in_specs=[hbm] * 9,
         out_specs=(vmem,) * 5,
         scratch_shapes=[
             pltpu.SMEM((groups, slots), jnp.int32),
@@ -257,13 +242,14 @@
             pltpu.VMEM((classes, width), F32),
             pltpu.VMEM((slots, size, size), BF16),
             pltpu.VMEM((rows, width), BF16),
+            pltpu.VMEM((1, width), BF16),
             pltpu.VMEM((table_rows, width), F32),
             pltpu.VMEM((rows + 2 * size, rows), F32),
-            pltpu.SemaphoreType.DMA((6 + 2 * (rows // size),)),
+            pltpu.SemaphoreType.DMA((7 + 2 * (rows // size),)),
         ],
         compiler_params=pltpu.CompilerParams(vmem_limit_bytes=16 * 2**20),
         name="messages",
-    )(*in_hbm(tile_rows, tile_cols, tile_live.T, labels, label_table, tiles, features, weights))
+    )(*in_hbm(tile_rows, tile_cols, tile_live.T, labels, label_table, tiles, features, gains, weights))
 
     beside = [(i, i ^ 1) for i in range(shard_count)]
     apart = [(i, (i + 1) % shard_count) for i in range(1, shard_count, 2)]
@@ -273,19 +259,19 @@
     far = lax.ppermute(far, "shard", apart)
     near = lax.ppermute(near, "shard", beside)
 
-    aggregate, own_weight, gain, half_gain, head_parts = pl.pallas_call(
+    aggregate, own_weight, half_gain, head_parts = pl.pallas_call(
         waiting_kernel,
         out_shape=(
             jax.ShapeDtypeStruct((rows + 2 * size, width), F32),
             jax.ShapeDtypeStruct((depth, width), BF16),
-            jax.ShapeDtypeStruct((1, width), BF16),
             jax.ShapeDtypeStruct((1, width), F32),
             jax.ShapeDtypeStruct((PAD, width), BF16),
         ),
         in_specs=[vmem] * 2 + [hbm] * 3,
-        out_specs=(vmem,) * 5,
+        out_specs=(vmem,) * 4,
         scratch_shapes=[
             pltpu.VMEM((1, width), F32),
+            pltpu.VMEM((1, width), BF16),
             pltpu.VMEM((PAD, width), F32),
             pltpu.SemaphoreType.DMA((3,)),
         ],
@@ -294,35 +280,32 @@
         name="waiting",
     )(adjacency, state, *in_hbm(head_weight.reshape(1, width), gains, weights))
 
-    other_gain = lax.ppermute(gain, "section", across)
-    near_blocks = pl.pallas_call(
+    near_aggregate = pl.pallas_call(
         near_kernel,
         out_shape=jax.ShapeDtypeStruct((2 * size, width), BF16),
-        in_specs=[vmem] * 5,
+        in_specs=[vmem] * 2,
         out_specs=vmem,
         compiler_params=pltpu.CompilerParams(vmem_limit_bytes=16 * 2**20),
         name="beside",
-    )(state, near, aggregate, own_weight, half_gain)
-
-    crossed, near_blocks, other_gain = lax.optimization_barrier((crossed, near_blocks, other_gain))
+    )(near, aggregate)
+
+    crossed, near_aggregate = lax.optimization_barrier((crossed, near_aggregate))
     relayed = lax.ppermute(crossed, "shard", beside)
 
     return pl.pallas_call(
         second_kernel,
         out_shape=jax.ShapeDtypeStruct((1, rows), F32),
-        in_specs=[vmem] * 12,
+        in_specs=[vmem] * 11,
         out_specs=vmem,
         scratch_shapes=[
             pltpu.VMEM((2, depth, width), BF16),
-            pltpu.VMEM((rows + 2 * size, width), BF16),
             pltpu.VMEM((rows + 2 * size, width), BF16),
             pltpu.VMEM((rows + 2 * size, width), BF16),
         ],
         compiler_params=pltpu.CompilerParams(vmem_limit_bytes=32 * 2**20),
         name="layers",
     )(
-        adjacency, state, far, near, other_gain, crossed, relayed,
-        near_blocks, aggregate, own_weight, half_gain, head_parts,
+        adjacency, state, far, near, crossed, relayed, near_aggregate, aggregate, own_weight, half_gain, head_parts,
     )
 
 

time: 16.7 us -> 15.6 us (0.934)
  Pallas kernels: 5.27 us -> 4.68 us
  starting transfers between devices: 7.29 us -> 6.76 us
    ppermute x1 -> x0, waiting for transfers between devices: 2.42 us -> none  [paired(): other_gain = lax.ppermute(gain, 'section', across)]
    ppermute x1, waiting for transfers between devices: 0.55 us -> 2.47 us  [paired(): far = lax.ppermute(far, 'shard', apart)]
    ppermute x1, waiting for transfers between devices: 0.01 us -> 0.99 us  [paired(): crossed = lax.ppermute(crossing, 'section', across)]
    ppermute x1, waiting for transfers between devices: 0.99 us -> 0.01 us  [paired(): relayed = lax.ppermute(crossed, 'shard', beside)]
    ppermute x1 -> x0, starting transfers between devices: 0.57 us -> none  [paired(): other_gain = lax.ppermute(gain, 'section', across)]
    ppermute x1, waiting for transfers between devices: 0.01 us -> 0.49 us  [paired(): near = lax.ppermute(near, 'shard', beside)]
    pallas_call x1, Pallas kernels: 0.64 us -> 0.18 us  [paired(): pl.pallas_call(near_kernel, out_shape=jax.ShapeDtypeStruct((2 * size, wid...]
  transfers between devices with their start and end apart: 5 -> 4, of which waited for: 3 -> 3; matrix products, arithmetic and copies ran while one was open for 0% -> 0% of each run, Pallas kernels for 10% -> 8%
where the time goes in v1:
time: 15.6 us; the launch traced here: 15.4 us
  starting transfers between devices  6.76 us (43%)
  Pallas kernels  4.68 us (30%)
  waiting for transfers between devices  3.95 us (25%)
    ppermute x1, starting transfers between devices, paired(): far = lax.ppermute(far, 'shard', apart)  3.72 us
    ppermute x1, starting transfers between devices, paired(): crossed = lax.ppermute(crossing, 'section', across)  3.03 us
    ppermute x1, waiting for transfers between devices, paired(): far = lax.ppermute(far, 'shard', apart)  2.47 us
    pallas_call x1, Pallas kernels, paired(): pl.pallas_call(second_kernel, out_shape=jax.ShapeDtypeStruct((1, rows), F...  1.94 us
    pallas_call x1, Pallas kernels, paired(): pl.pallas_call(first_kernel, out_shape=(message, message, jax.ShapeDtypeS...  1.47 us
    pallas_call x1, Pallas kernels, paired(): pl.pallas_call(waiting_kernel, out_shape=(jax.ShapeDtypeStruct((rows + 2...  1.08 us
    ppermute x1, waiting for transfers between devices, paired(): crossed = lax.ppermute(crossing, 'section', across)  0.99 us
    ppermute x1, waiting for transfers between devices, paired(): near = lax.ppermute(near, 'shard', beside)  0.49 us
  transfers between devices with their start and end apart: 4, of which 3 were waited for; matrix products, arithmetic and copies ran while one was open for 0% of the time, Pallas kernels for 8%

profile of v1, /device:TPU:0, one launch (start us, length us, event | category | flops | bytes accessed | tf_op | source)
XLA Modules:
  0.0 15.4 jit_solution(2102405886393196663)
XLA Ops:
  0.0 1.5 %messages.1 = (bf16[128,1152]{1,0:T(8,128)(2,1)S(1)}, bf16[128,1152]{1,0:T(8,128)(2,1)S(1)}, bf16[264,512]{1,0:T(8,128)(2,1)S(1)}, bf16[256,512]{1,0:T(8,128)(2,1)S(1)}, bf16[512,256]{1,0:T(8,128)(2,1)S(1)}) custom-call(s32[2,6]{1,0:T(2,128)} %tile_rows.1, s32[2,6]{1,0:T(2,128)} %tile_cols.1, s32[1,2]{1,0:T(1,128)} %bitcast.2, s32[2,256]{1,0:T(2,128)} %labels.1, ...), custom_call_target="tpu_custom_call" | custom-call | tf_op jit(solution)/shard_map/messages/pallas_call | solution.py:226
  1.5 3.0 %collective-permute-start.2 = (bf16[264,512]{1,0:T(8,128)(2,1)S(1)}, bf16[264,512]{1,0:T(8,128)(2,1)S(1)}, u32[]{:S(2)}, u32[]{:S(2)}) collective-permute-start(bf16[264,512]{1,0:T(8,128)(2,1)S(1)} %get-tuple-element.20), channel_id=1, source_target_pairs={{0,16},{16,0},{1,17},{17,1},{2,18},{18,2},{3,19},{19,3},{4,20},{20... | collective-permute-start | bytes 811016 | tf_op jit(solution)/shard_map/ppermute | solution.py:258
  4.5 3.7 %collective-permute-start = (bf16[128,1152]{1,0:T(8,128)(2,1)S(1)}, bf16[128,1152]{1,0:T(8,128)(2,1)S(1)}, u32[]{:S(2)}, u32[]{:S(2)}) collective-permute-start(bf16[128,1152]{1,0:T(8,128)(2,1)S(1)} %get-tuple-element.18), channel_id=1, source_target_pairs={{1,2},{3,4},{5,6},{7,8},{9,10},{11,12},{13,14},{15,0},{2,1},{4,3},... | collective-permute-start | bytes 884744 | tf_op jit(solution)/shard_map/ppermute | solution.py:259
  8.2 0.0 collective-permute-start.1
  8.2 1.1 %waiting.1 = (f32[512,512]{1,0:T(8,128)S(1)}, bf16[512,512]{1,0:T(8,128)(2,1)S(1)}, f32[1,512]{1,0:T(1,128)S(1)}, bf16[16,512]{1,0:T(8,128)(2,1)S(1)}) custom-call(bf16[512,256]{1,0:T(8,128)(2,1)S(1)} %get-tuple-element.16.adjacency, bf16[256,512]{1,0:T(8,128)(2,1)S(1)} %get-tuple-element.17.state, f32[1,512]{1,0:T(1,128)} %bitcast.3, bf16[1,512]{1,0:T(2,128)(2,1)} %gains.3, ...), custom_call_target="tpu_custom_call" | custom-call | flops 4000000000 | bytes 1048576 | tf_op jit(solution)/shard_map/waiting/pallas_call | solution.py:262
  9.3 0.5 %collective-permute-done.1.near = bf16[128,1152]{1,0:T(8,128)(2,1)S(1)} collective-permute-done((bf16[128,1152]{1,0:T(8,128)(2,1)S(1)}, bf16[128,1152]{1,0:T(8,128)(2,1)S(1)}, u32[]{:S(2)}, u32[]{:S(2)}) %collective-permute-start.1) | collective-permute-done | bytes 294944 | tf_op jit(solution)/shard_map/ppermute | solution.py:260
  9.8 0.2 %beside.1.near_aggregate = bf16[256,512]{1,0:T(8,128)(2,1)S(1)} custom-call(bf16[128,1152]{1,0:T(8,128)(2,1)S(1)} %collective-permute-done.1.near, f32[512,512]{1,0:T(8,128)S(1)} %get-tuple-element.21.aggregate), custom_call_target="tpu_custom_call" | custom-call | tf_op jit(solution)/shard_map/beside/pallas_call | solution.py:283
  10.0 1.0 %collective-permute-done.2.crossed = bf16[264,512]{1,0:T(8,128)(2,1)S(1)} collective-permute-done((bf16[264,512]{1,0:T(8,128)(2,1)S(1)}, bf16[264,512]{1,0:T(8,128)(2,1)S(1)}, u32[]{:S(2)}, u32[]{:S(2)}) %collective-permute-start.2) | collective-permute-done | bytes 270368 | tf_op jit(solution)/shard_map/ppermute | solution.py:258
  11.0 0.0 collective-permute-start.3
  11.0 2.5 %collective-permute-done.far = bf16[128,1152]{1,0:T(8,128)(2,1)S(1)} collective-permute-done((bf16[128,1152]{1,0:T(8,128)(2,1)S(1)}, bf16[128,1152]{1,0:T(8,128)(2,1)S(1)}, u32[]{:S(2)}, u32[]{:S(2)}) %collective-permute-start) | collective-permute-done | bytes 294944 | tf_op jit(solution)/shard_map/ppermute | solution.py:259
  13.5 0.0 collective-permute-done.3.relayed
  13.5 1.9 %layers.1 = f32[1,256]{1,0:T(1,128)} custom-call(bf16[512,256]{1,0:T(8,128)(2,1)S(1)} %get-tuple-element.16.adjacency, bf16[256,512]{1,0:T(8,128)(2,1)S(1)} %get-tuple-element.17.state, bf16[128,1152]{1,0:T(8,128)(2,1)S(1)} %collective-permute-done.far, bf16[128,1152]{1,0:T(8,128)(2,1)S(1)} %collective-permute-done.1.near, ...), custom_call_target="tpu_custom_call" | custom-call | tf_op jit(solution)/shard_map/layers/pallas_call | solution.py:295
Async XLA Ops:
  1.5 9.5 %collective-permute-start.2 = (bf16[264,512]{1,0:T(8,128)(2,1)S(1)}, bf16[264,512]{1,0:T(8,128)(2,1)S(1)}, u32[]{:S(2)}, u32[]{:S(2)}) collective-permute-start(bf16[264,512]{1,0:T(8,128)(2,1)S(1)} %get-tuple-element.20), channel_id=1, source_target_pairs={{0,16},{16,0},{1,17},{17,1},{2,18},{18,2},{3,19},{19,3},{4,20},{20... | collective-permute-start | bytes 811016 | tf_op jit(solution)/shard_map/ppermute | solution.py:258
  4.5 9.0 %collective-permute-start = (bf16[128,1152]{1,0:T(8,128)(2,1)S(1)}, bf16[128,1152]{1,0:T(8,128)(2,1)S(1)}, u32[]{:S(2)}, u32[]{:S(2)}) collective-permute-start(bf16[128,1152]{1,0:T(8,128)(2,1)S(1)} %get-tuple-element.18), channel_id=1, source_target_pairs={{1,2},{3,4},{5,6},{7,8},{9,10},{11,12},{13,14},{15,0},{2,1},{4,3},... | collective-permute-start | bytes 884744 | tf_op jit(solution)/shard_map/ppermute | solution.py:259
  8.2 1.6 %collective-permute-start.1 = (bf16[128,1152]{1,0:T(8,128)(2,1)S(1)}, bf16[128,1152]{1,0:T(8,128)(2,1)S(1)}, u32[]{:S(2)}, u32[]{:S(2)}) collective-permute-start(bf16[128,1152]{1,0:T(8,128)(2,1)S(1)} %get-tuple-element.19), channel_id=1, source_target_pairs={{0,1},{1,0},{2,3},{3,2},{4,5},{5,4},{6,7},{7,6},{8,9},{9,8},{10,11... | collective-permute-start | bytes 884744 | tf_op jit(solution)/shard_map/ppermute | solution.py:260
  11.0 2.5 %collective-permute-start.3 = (bf16[264,512]{1,0:T(8,128)(2,1)S(1)}, bf16[264,512]{1,0:T(8,128)(2,1)S(1)}, u32[]{:S(2)}, u32[]{:S(2)}) collective-permute-start(bf16[264,512]{1,0:T(8,128)(2,1)S(1)} %collective-permute-done.2.crossed), channel_id=1, source_target_pairs={{0,1},{1,0},{2,3},{3,2},{4,5},{5,4},{6,7},{7,6},{8,9},{9,8},{10,11... | collective-permute-start | bytes 811016 | tf_op jit(solution)/shard_map/ppermute | solution.py:293
